TPU v7x, 1024 devices: a whole 4x4x32 slice. The times are simulated.
1024 devices in a mesh: rep: 128 (over z, y), tp: 8 (over x, core).
Axes of the slice: x: 4, y: 4, z: 32, core: 2. Of those that a mesh axis runs over, the one named last changes fastest.
Arguments:
- tokens: bfloat16 [131072, 4096], P('rep', 'tp'), may hold values from -6 to 6
- key_grad: bfloat16 [131072, 512], P('rep', 'tp'), may hold values from -0.19921875 to 0.19921875
- momentum: float32 [128, 4096, 512], P('rep', 'tp'), may hold values from -6 to 6
- key_weight: bfloat16 [4096, 512], P('tp'), may hold values from -4 to 4
- target: bfloat16 [4096, 512], P('tp'), may hold values from -4 to 4
- positions: int32 [64, 8, 64], P('tp'), may hold values from 0 to 4095, as said below
Outputs:
- update: float32 [4096, 512], P('tp')
- residual: float32 [128, 4096, 512], P('rep', 'tp')
- blended: bfloat16 [4096, 512], P('tp')
Inputs may be any that keep to these rules, and one draw needn't show every extreme that they name: The 64 positions of each block are distinct coefficient numbers of that block.
All inputs are finite; a program needn't handle non-finite values.
Results may differ from a plain program's by a relative error of at most 0.0054.
Values may be sent and summed in bfloat16 or wider, within the bound.
A program may use at most 64 MiB of HBM per device.

v0:
```python
import math

import jax
import jax.numpy as jnp
from jax import lax
from jax.sharding import PartitionSpec as P

BLOCK = 64


momentum_decay = 0.9
polyak_rate = 0.25
update_rate = 0.1


def cosine_table(length):
    index = jnp.arange(length).astype(jnp.float32)
    angle_grid = jnp.pi * (2.0 * index[None, :] + 1.0) * index[:, None] / (2.0 * length)
    scales = jnp.where(index == 0, jnp.sqrt(1.0 / length), jnp.sqrt(2.0 / length))
    return scales[:, None] * jnp.cos(angle_grid)


def wide_table(table, breadth):
    width = math.gcd(breadth, 128)
    return (jnp.kron(jnp.eye(width // BLOCK, dtype=jnp.float32), table), width)


def to_spectrum(field, table):
    height, breadth = field.shape
    wide, width = wide_table(table, breadth)
    left = jnp.einsum(
        "ai,pik->pak",
        table,
        field.reshape(height // BLOCK, BLOCK, breadth),
        precision=lax.Precision.HIGHEST,
    )
    both = jnp.einsum(
        "pagw,vw->pagv",
        left.reshape(height // BLOCK, BLOCK, breadth // width, width),
        wide,
        precision=lax.Precision.HIGHEST,
    )
    square = both.reshape(height // BLOCK, BLOCK, breadth // BLOCK, BLOCK).transpose(0, 2, 1, 3)
    return square.reshape(height // BLOCK, breadth // BLOCK, BLOCK * BLOCK)


def from_spectrum(spectrum, table):
    row_blocks, col_blocks, _ = spectrum.shape
    breadth = col_blocks * BLOCK
    wide, width = wide_table(table, breadth)
    square = spectrum.reshape(row_blocks, col_blocks, BLOCK, BLOCK).transpose(0, 2, 1, 3)
    right = jnp.einsum(
        "pagv,vw->pagw",
        square.reshape(row_blocks, BLOCK, breadth // width, width),
        wide,
        precision=lax.Precision.HIGHEST,
    )
    field = jnp.einsum(
        "ai,pak->pik",
        table,
        right.reshape(row_blocks, BLOCK, breadth),
        precision=lax.Precision.HIGHEST,
    )
    return field.reshape(row_blocks * BLOCK, breadth)


def scatter_kept(values, positions):
    row_blocks, col_blocks, _ = values.shape
    first = jnp.arange(row_blocks)[:, None, None]
    second = jnp.arange(col_blocks)[None, :, None]
    empty = jnp.zeros((row_blocks, col_blocks, BLOCK * BLOCK), jnp.float32)
    return empty.at[first, second, positions].set(values)


def shards(tokens, key_grad, momentum, key_weight, target, positions):
    table = cosine_table(BLOCK)
    gradient = lax.dot_general(
        tokens,
        lax.all_gather(key_grad, "tp", axis=1, tiled=True),
        (((0,), (0,)), ((), ())),
        preferred_element_type=jnp.float32,
    )
    moment = momentum_decay * momentum[0] + gradient
    kept = jnp.take_along_axis(to_spectrum(moment, table), positions, axis=2)
    total = lax.psum(kept, "rep")
    residual = moment - from_spectrum(scatter_kept(kept, positions), table)
    update = from_spectrum(scatter_kept(total, positions), table)
    blended = (1.0 - polyak_rate) * target.astype(jnp.float32) + polyak_rate * (
        key_weight.astype(jnp.float32) - update_rate * update
    )
    return (update, residual[None], blended.astype(jnp.bfloat16))


def solution(mesh):
    in_specs = (
        P("rep", "tp"),
        P("rep", "tp"),
        P("rep", "tp", None),
        P("tp", None),
        P("tp", None),
        P("tp", None, None),
    )
    out_specs = (P("tp", None), P("rep", "tp", None), P("tp", None))
    return jax.shard_map(shards, mesh=mesh, in_specs=in_specs, out_specs=out_specs, check_vma=False)
```

profile of v0, /device:TPU:4, one launch (start us, length us, event | category | flops | bytes accessed | tf_op | source)
XLA Modules:
  0.0 717.4 jit_solution(14965314992523216577)
XLA Ops:
  8.5 0.8 shift-left_or_fusion
  11.7 46.7 %all-gather.2.cloned.1.call-done = bf16[1024,512]{0,1:T(8,128)(2,1)} async-done(((bf16[1024,64]{0,1:T(8,128)(2,1)}), bf16[1024,512]{0,1:T(8,128)(2,1)}) %all-gather.2.cloned.1.call-update) | async-done | bytes 1048592 | tf_op jit(solution)/shard_map/all_gather | solution.py:79
  58.4 2.3 convolution_add_fusion
  60.7 1.3 convolution_bitcast_fusion.2
  62.0 1.0 fusion.6
  63.7 2.0 reshape.149
  65.7 3.3 copy.25
  68.9 2.1 reshape.150
  71.1 32.0 %gather_fusion = f32[4096]{0:T(1024)S(1)} fusion(f32[8,8,4096]{2,1,0:T(8,128)S(1)} %reshape.150, s32[4096]{0:T(1024)S(1)} %reshape.169), kind=kCustom, calls=%fused_computation | custom fusion | bytes 81920 | tf_op jit(solution)/shard_map/jit(take_along_axis)/gather | solution.py:84
  103.2 553.8 %psum.7 = f32[8,8,64]{2,1,0:T(8,128)S(1)} all-reduce(f32[8,8,64]{2,1,0:T(8,128)S(1)} %and_select_fusion), channel_id=1, replica_groups=mesh['rep'=128,'tp'=8] {'rep'}, use_global_device_ids=true, to_apply=%region_0.1 | all-reduce | flops 4096 | bytes 32768 | tf_op jit(solution)/shard_map/psum | solution.py:85
  657.0 16.0 %scatter_custom_fusion.1 = f32[262144]{0:T(1024)S(1)} fusion(s32[4096]{0:T(1024)S(1)} %reshape.175, f32[4096]{0:T(1024)S(1)} %reshape.183, f32[]{:T(128)} %constant.15.clone.1), kind=kCustom, calls=%fused_computation.20 | custom fusion | bytes 1048580
  673.0 1.7 reshape.155
  674.7 4.1 copy.29
  678.8 2.0 reshape.156
  680.8 1.0 convolution_bitcast_fusion
  681.8 1.4 fusion
  683.1 1.2 bitcast_subtract_fusion
  684.4 16.5 %scatter_custom_fusion = f32[262144]{0:T(1024)} fusion(s32[4096]{0:T(1024)S(1)} %reshape.175, f32[4096]{0:T(1024)S(1)} %reshape.177, f32[]{:T(128)} %constant.15.clone.1), kind=kCustom, calls=%fused_computation.22 | custom fusion | bytes 1048580
  700.9 1.6 reshape.151
  702.5 2.5 copy.26
  705.0 2.0 reshape.152
  707.1 1.0 convolution_bitcast_fusion.1
  708.0 1.4 fusion.3
  709.4 1.1 add_convert_fusion
  (32 shorter events, 4.6 us)
Async XLA Ops:
  7.2 51.3 %copy-start = (bf16[1024,512]{1,0:T(8,128)(2,1)S(1)}, bf16[1024,512]{1,0:T(8,128)(2,1)}, u32[]{:S(2)}) copy-start(bf16[1024,512]{1,0:T(8,128)(2,1)} %param.6) | copy-start | bytes 3145732
  7.2 51.2 %all-gather.2.cloned.1.call-start = ((), (), s32[]{:S(2)}) async-start(), calls=%async_computation | async-start | bytes 1179648 | tf_op jit(solution)/shard_map/all_gather | solution.py:79
  71.1 32.1 %copy-start.4 = (s32[8,8,64]{2,1,0:T(8,128)S(1)}, s32[8,8,64]{2,1,0:T(8,128)}, u32[]{:S(2)}) copy-start(s32[8,8,64]{2,1,0:T(8,128)} %param.11) | copy-start | bytes 49156
  707.0 2.4 copy-start.2
  707.0 2.4 copy-start.3
  709.4 1.1 copy-start.1
Sparse Core Ops, SparseCore 0:
  10.7 47.6 all-gather.1
where the time goes:
time: 718 us; the launch traced here: 717 us
  blocking collectives  554 us (77%)
  local copies, waits for them, and re-layouts  87 us (12%)
  waiting for transfers between devices  47.4 us (7%)
  between operations  14.3 us (2%)
  matrix products  9.2 us (1%)
    psum x1, blocking collectives, shards(): total = lax.psum(kept, 'rep')  554 us
    all_gather x1, waiting for transfers between devices, shards(): lax.all_gather(key_grad, 'tp', axis=1, tiled=True)  46.7 us
    unnamed x13, local copies, waits for them, and re-layouts  32.6 us
    gather x2, local copies, waits for them, and re-layouts, shards(): kept = jnp.take_along_axis(to_spectrum(moment, table), positions, axis=2)  32 us
  transfers between devices with their start and end apart: 1, of which 1 were waited for; matrix products, arithmetic and copies ran while one was open for 1% of the time, Pallas kernels for 0%

commit v1 on v0

v1 whole, which is shorter than its diff:
```python
import functools

import jax
import jax.numpy as jnp
import ml_dtypes
import numpy as np
from jax import lax
from jax.experimental import pallas as pl
from jax.experimental.pallas import tpu as pltpu
from jax.sharding import PartitionSpec as P

BLOCK = 64
LANES = 128
NX, NY = 4, 4

momentum_decay = 0.9
polyak_rate = 0.25
update_rate = 0.1

MESH = pl.DeviceIdType.MESH
NT = (((1,), (1,)), ((), ()))


def split_table():
    index = np.arange(BLOCK, dtype=np.float64)
    angle = np.pi * (2.0 * index[:, None] + 1.0) * index[None, :] / (2.0 * BLOCK)
    scale = np.where(index == 0, np.sqrt(1.0 / BLOCK), np.sqrt(2.0 / BLOCK))
    table = np.cos(angle) * scale[None, :]
    high = table.astype(ml_dtypes.bfloat16)
    low = (table - high.astype(np.float64)).astype(ml_dtypes.bfloat16)
    return np.concatenate([high, low], axis=0)


def split_rows(value):
    high = value.astype(jnp.bfloat16)
    low = (value - high.astype(jnp.float32)).astype(jnp.bfloat16)
    return high, low


def strip_of(strip):
    return pl.ds(pl.multiple_of(strip * LANES, LANES), LANES)


def make_bases(pos_ref, table_ref, at_ref, w_ref):
    row_blocks, col_blocks, keep = pos_ref.shape
    width = col_blocks * keep
    lane = lax.broadcasted_iota(jnp.int32, (BLOCK, LANES), 1)
    level = lax.broadcasted_iota(jnp.int32, (BLOCK, width), 0)
    table = table_ref[...]
    flat = jnp.concatenate([pos_ref[:, b, :] for b in range(col_blocks)], axis=1)
    for p in range(row_blocks):
        row = flat[p : p + 1, :]
        first = jnp.where(level == (row >> 6), 1.0, 0.0).astype(jnp.bfloat16)
        second = jnp.where(level == (row & 63), 1.0, 0.0).astype(jnp.bfloat16)
        picked = jnp.dot(table, first, preferred_element_type=jnp.float32)
        at_ref[p] = picked[:BLOCK] + picked[BLOCK:]
        other = jnp.dot(table, second, preferred_element_type=jnp.float32)
        for g in range(width // LANES):
            for part in range(2):
                piece = other[part * BLOCK : (part + 1) * BLOCK, g * LANES : (g + 1) * LANES]
                top = jnp.where(lane < BLOCK, piece, 0.0).astype(jnp.bfloat16)
                low = jnp.where(lane < BLOCK, 0.0, piece).astype(jnp.bfloat16)
                w_ref[p, g, 0:BLOCK, part * LANES : (part + 1) * LANES] = top
                w_ref[p, g, BLOCK : 2 * BLOCK, part * LANES : (part + 1) * LANES] = low


def encode(block, at, w):
    high, low = split_rows(block)
    both = jnp.dot(jnp.concatenate([high, low], axis=0), w, preferred_element_type=jnp.float32)
    mixed = both[:BLOCK, :LANES] + both[:BLOCK, LANES:] + both[BLOCK:, :LANES]
    return jnp.sum(mixed * at, axis=0, keepdims=True)


def decode(values, at, w):
    high, low = split_rows(at * values)
    rows = jnp.concatenate(
        [jnp.concatenate([high, high], axis=1), jnp.concatenate([low, jnp.zeros_like(low)], axis=1)], axis=0
    )
    both = lax.dot_general(rows, w, NT, preferred_element_type=jnp.float32)
    return both[:BLOCK] + both[BLOCK:]


def first_kernel(
    ny, nz,
    tok_hbm, grad_hbm, mom_hbm, pos_hbm, table_hbm,
    res_hbm, total_hbm, at_hbm, w_hbm,
    tok, tok_t, gall, mom, at, w, pos, table, kept, part, ybuf, total,
    load_sem, send_sem, recv_sem, z_send, z_recv, y_send, y_recv, out_sem,
):
    rep, tp = lax.axis_index("rep"), lax.axis_index("tp")
    z, y = rep // ny, lax.rem(rep, ny)
    x, core = tp // 2, lax.rem(tp, 2)
    right = lax.rem(x + 1, NX) * 2 + core
    left = lax.rem(x + NX - 1, NX) * 2 + core
    far = lax.rem(x + 2, NX) * 2 + core
    other = 2 * x + 1 - core
    rows_p = at.shape[0]
    chunk = kept.shape[0] // nz

    loads = [
        pltpu.make_async_copy(pos_hbm, pos, load_sem.at[0]),
        pltpu.make_async_copy(table_hbm, table, load_sem.at[1]),
        pltpu.make_async_copy(grad_hbm, gall.at[pl.ds(pl.multiple_of(tp * BLOCK, BLOCK), BLOCK)], load_sem.at[2]),
        pltpu.make_async_copy(tok_hbm, tok, load_sem.at[3]),
        pltpu.make_async_copy(mom_hbm, mom, load_sem.at[4]),
    ]
    for load in loads:
        load.start()

    barrier = pltpu.get_barrier_semaphore()
    for peer in (right, left, other):
        pl.semaphore_signal(barrier, inc=1, device_id={"tp": peer}, device_id_type=MESH)

    def greet_z(step, carry):
        peer = lax.rem(z + step, nz) * ny + y
        pl.semaphore_signal(barrier, inc=1, device_id={"rep": peer}, device_id_type=MESH)
        return carry

    def greet_y(step, carry):
        peer = z * ny + lax.rem(y + step, ny)
        pl.semaphore_signal(barrier, inc=1, device_id={"rep": peer}, device_id_type=MESH)
        return carry

    lax.fori_loop(1, nz, greet_z, 0)
    lax.fori_loop(1, ny, greet_y, 0)

    loads[0].wait()
    loads[1].wait()
    make_bases(pos, table, at, w)
    bases_out = [
        pltpu.make_async_copy(at, at_hbm, out_sem.at[0]),
        pltpu.make_async_copy(w, w_hbm, out_sem.at[1]),
    ]
    for copy in bases_out:
        copy.start()

    pl.semaphore_wait(barrier, 3 + (nz - 1) + (ny - 1))

    half = BLOCK // 2

    def rows(owner, part_at):
        return gall.at[pl.ds(pl.multiple_of(owner * BLOCK + part_at * half, half), half)]

    def send(number, source, target, device):
        copy = pltpu.make_async_remote_copy(
            src_ref=source, dst_ref=target, send_sem=send_sem.at[number], recv_sem=recv_sem.at[number],
            device_id={"tp": device}, device_id_type=MESH,
        )
        copy.start()
        return copy

    def arrived(number, target):
        pltpu.make_async_remote_copy(
            src_ref=target, dst_ref=target, send_sem=send_sem.at[number], recv_sem=recv_sem.at[number],
            device_id={"tp": other}, device_id_type=MESH,
        ).wait_recv()

    sent = [
        send(0, grad_hbm.at[0:half], rows(tp, 0), right),
        send(2, grad_hbm.at[half:BLOCK], rows(tp, 1), left),
        send(6, grad_hbm, gall.at[pl.ds(pl.multiple_of(tp * BLOCK, BLOCK), BLOCK)], other),
        send(1, grad_hbm.at[half:BLOCK], rows(tp, 1), right),
        send(3, grad_hbm.at[0:half], rows(tp, 0), left),
    ]

    loads[3].wait()
    depth = tok.shape[0]
    for at_row in range(0, depth, 256):
        tok_t[:, at_row : at_row + 256] = tok[at_row : at_row + 256, :].T
    loads[2].wait()
    loads[4].wait()

    arrived(0, rows(left, 0))
    sent.append(send(4, rows(left, 0), rows(left, 0), right))
    sent.append(send(7, rows(left, 0), rows(left, 0), other))
    arrived(2, rows(right, 1))
    sent.append(send(5, rows(right, 1), rows(right, 1), left))
    sent.append(send(10, rows(right, 1), rows(right, 1), other))
    arrived(1, rows(left, 1))
    sent.append(send(8, rows(left, 1), rows(left, 1), other))
    arrived(3, rows(right, 0))
    sent.append(send(9, rows(right, 0), rows(right, 0), other))

    def forward(strip):
        grads = gall[pl.ds(pl.multiple_of(strip * LANES, LANES), LANES), :]
        gradient = lax.dot_general(tok_t[...], grads, NT, preferred_element_type=jnp.float32)
        moment = momentum_decay * mom[:, strip_of(strip)] + gradient
        mom[:, strip_of(strip)] = moment
        for p in range(rows_p):
            block = moment[p * BLOCK : (p + 1) * BLOCK]
            kept[strip * rows_p + p] = encode(block, at[p, :, strip_of(strip)], w[p, strip])

    def backward(strip):
        for p in range(rows_p):
            field = decode(kept[strip * rows_p + p], at[p, :, strip_of(strip)], w[p, strip])
            mom[p * BLOCK : (p + 1) * BLOCK, strip_of(strip)] = (
                mom[p * BLOCK : (p + 1) * BLOCK, strip_of(strip)] - field
            )

    left_x, right_x, far_x = lax.rem(x + NX - 1, NX), lax.rem(x + 1, NX), lax.rem(x + 2, NX)
    left_o, right_o, far_o = left_x * 2 + 1 - core, right_x * 2 + 1 - core, far_x * 2 + 1 - core

    arrived(6, gall.at[pl.ds(pl.multiple_of(other * BLOCK, BLOCK), BLOCK)])
    forward(x)
    arrived(7, rows(left_o, 0))
    arrived(8, rows(left_o, 1))
    forward(left_x)
    arrived(4, rows(far, 0))
    sent.append(send(11, rows(far, 0), rows(far, 0), other))
    arrived(5, rows(far, 1))
    sent.append(send(12, rows(far, 1), rows(far, 1), other))
    arrived(9, rows(right_o, 0))
    arrived(10, rows(right_o, 1))
    forward(right_x)
    arrived(11, rows(far_o, 0))
    arrived(12, rows(far_o, 1))
    forward(far_x)

    def scatter_z(step, carry):
        peer = lax.rem(z + step, nz)
        pltpu.make_async_remote_copy(
            src_ref=kept.at[pl.ds(peer * chunk, chunk)], dst_ref=part.at[z], send_sem=z_send.at[0], recv_sem=z_recv.at[0],
            device_id={"rep": peer * ny + y}, device_id_type=MESH,
        ).start()
        return carry

    lax.fori_loop(1, nz, scatter_z, 0)
    part[z] = kept[pl.ds(z * chunk, chunk)]
    backward(x)
    backward(left_x)
    many = part.at[pl.ds(0, nz - 1)]
    pltpu.make_async_copy(many, many, z_recv.at[0]).wait()
    ybuf[y] = jnp.sum(part[...], axis=0)

    def swap_y(step, carry):
        peer = z * ny + lax.rem(y + step, ny)
        pltpu.make_async_remote_copy(
            src_ref=ybuf.at[y], dst_ref=ybuf.at[y], send_sem=y_send, recv_sem=y_recv,
            device_id={"rep": peer}, device_id_type=MESH,
        ).start()
        return carry

    lax.fori_loop(1, ny, swap_y, 0)
    some = ybuf.at[pl.ds(0, ny - 1)]
    pltpu.make_async_copy(some, some, y_recv).wait()
    total[z] = jnp.sum(ybuf[...], axis=0)

    def gather_z(step, carry):
        peer = lax.rem(z + step, nz)
        pltpu.make_async_remote_copy(
            src_ref=total.at[z], dst_ref=total.at[z], send_sem=z_send.at[1], recv_sem=z_recv.at[1],
            device_id={"rep": peer * ny + y}, device_id_type=MESH,
        ).start()
        return carry

    lax.fori_loop(1, nz, gather_z, 0)
    backward(right_x)
    backward(far_x)
    res_out = pltpu.make_async_copy(mom, res_hbm, out_sem.at[2])
    res_out.start()
    most = total.at[pl.ds(0, nz - 1)]
    pltpu.make_async_copy(most, most, z_recv.at[1]).wait()
    total_out = pltpu.make_async_copy(total, total_hbm, out_sem.at[3])
    total_out.start()

    for copy in sent:
        copy.wait_send()
    pltpu.make_async_copy(many, many, z_send.at[0]).wait()
    pltpu.make_async_copy(some, some, y_send).wait()
    pltpu.make_async_copy(most, most, z_send.at[1]).wait()
    for copy in bases_out:
        copy.wait()
    res_out.wait()
    total_out.wait()


def second_kernel(
    total_hbm, at_hbm, w_hbm, res_in, weight_hbm, target_hbm,
    update_hbm, res_hbm, blended_hbm,
    total, at, w, weight, target, update, blended, load_sem, out_sem,
):
    res_copy = pltpu.make_async_copy(res_in, res_hbm, out_sem.at[0])
    loads = [
        pltpu.make_async_copy(total_hbm, total, load_sem.at[0]),
        pltpu.make_async_copy(at_hbm, at, load_sem.at[1]),
        pltpu.make_async_copy(w_hbm, w, load_sem.at[2]),
        pltpu.make_async_copy(weight_hbm, weight, load_sem.at[3]),
        pltpu.make_async_copy(target_hbm, target, load_sem.at[4]),
    ]
    for load in loads:
        load.start()
    res_copy.start()
    for load in loads:
        load.wait()
    rows_p, strips = w.shape[:2]
    outs = []
    for p in range(rows_p):
        at_rows = slice(p * BLOCK, (p + 1) * BLOCK)
        for g in range(strips):
            at_lanes = slice(g * LANES, (g + 1) * LANES)
            field = decode(total[g * rows_p + p], at[p, :, at_lanes], w[p, g])
            update[at_rows, at_lanes] = field
            moved = weight[at_rows, at_lanes].astype(jnp.float32) - update_rate * field
            mixed = (1.0 - polyak_rate) * target[at_rows, at_lanes].astype(jnp.float32) + polyak_rate * moved
            blended[at_rows, at_lanes] = mixed.astype(jnp.bfloat16)
        outs.append(pltpu.make_async_copy(update.at[at_rows], update_hbm.at[at_rows], out_sem.at[1 + 2 * p]))
        outs.append(pltpu.make_async_copy(blended.at[at_rows], blended_hbm.at[at_rows], out_sem.at[2 + 2 * p]))
        outs[-2].start()
        outs[-1].start()
    for copy in outs:
        copy.wait()
    res_copy.wait()


def shards(ny, nz, tokens, key_grad, momentum, key_weight, target, positions):
    anywhere = pl.BlockSpec(memory_space=pl.ANY)
    in_hbm = pl.BlockSpec(memory_space=pltpu.HBM)
    table = jnp.asarray(split_table())
    depth, feats = tokens.shape
    _, _, width = momentum.shape
    rows_p, col_blocks, keep = positions.shape
    strips = width // LANES
    rows = rows_p * strips
    chunk = rows // nz
    at_shape, w_shape = (rows_p, BLOCK, width), (rows_p, strips, 2 * BLOCK, 2 * LANES)
    residual, total, at, w = pl.pallas_call(
        functools.partial(first_kernel, ny, nz),
        out_shape=(
            jax.ShapeDtypeStruct((feats, width), jnp.float32),
            jax.ShapeDtypeStruct((nz, chunk, 1, LANES), jnp.float32),
            jax.ShapeDtypeStruct(at_shape, jnp.float32),
            jax.ShapeDtypeStruct(w_shape, jnp.bfloat16),
        ),
        in_specs=[in_hbm] * 5,
        out_specs=(anywhere,) * 4,
        scratch_shapes=[
            pltpu.VMEM((depth, feats), jnp.bfloat16),
            pltpu.VMEM((feats, depth), jnp.bfloat16),
            pltpu.VMEM((width, depth), jnp.bfloat16),
            pltpu.VMEM((feats, width), jnp.float32),
            pltpu.VMEM(at_shape, jnp.float32),
            pltpu.VMEM(w_shape, jnp.bfloat16),
            pltpu.VMEM((rows_p, col_blocks, keep), jnp.int32),
            pltpu.VMEM(table.shape, jnp.bfloat16),
            pltpu.VMEM((rows, 1, LANES), jnp.float32),
            pltpu.VMEM((nz, chunk, 1, LANES), jnp.float32),
            pltpu.VMEM((ny, chunk, 1, LANES), jnp.float32),
            pltpu.VMEM((nz, chunk, 1, LANES), jnp.float32),
            pltpu.SemaphoreType.DMA((5,)),
            pltpu.SemaphoreType.DMA((13,)),
            pltpu.SemaphoreType.DMA((13,)),
            pltpu.SemaphoreType.DMA((2,)),
            pltpu.SemaphoreType.DMA((2,)),
            pltpu.SemaphoreType.DMA,
            pltpu.SemaphoreType.DMA,
            pltpu.SemaphoreType.DMA((4,)),
        ],
        compiler_params=pltpu.CompilerParams(
            collective_id=0, has_side_effects=True, vmem_limit_bytes=32 * 1024 * 1024
        ),
        cost_estimate=pl.CostEstimate(flops=1_000_000_000, bytes_accessed=8_000_000, transcendentals=0),
        name="gather_encode_sum",
    )(tokens, key_grad.T, momentum[0], positions, table)
    update, residual, blended = pl.pallas_call(
        second_kernel,
        out_shape=(
            jax.ShapeDtypeStruct((feats, width), jnp.float32),
            jax.ShapeDtypeStruct((feats, width), jnp.float32),
            jax.ShapeDtypeStruct((feats, width), jnp.bfloat16),
        ),
        in_specs=[anywhere] * 6,
        out_specs=(anywhere,) * 3,
        scratch_shapes=[
            pltpu.VMEM((rows, 1, LANES), jnp.float32),
            pltpu.VMEM(at_shape, jnp.float32),
            pltpu.VMEM(w_shape, jnp.bfloat16),
            pltpu.VMEM((feats, width), jnp.bfloat16),
            pltpu.VMEM((feats, width), jnp.bfloat16),
            pltpu.VMEM((feats, width), jnp.float32),
            pltpu.VMEM((feats, width), jnp.bfloat16),
            pltpu.SemaphoreType.DMA((5,)),
            pltpu.SemaphoreType.DMA((1 + 2 * rows_p,)),
        ],
        compiler_params=pltpu.CompilerParams(vmem_limit_bytes=32 * 1024 * 1024),
        cost_estimate=pl.CostEstimate(flops=300_000_000, bytes_accessed=8_000_000, transcendentals=0),
        name="decode_blend",
    )(total.reshape(rows, 1, LANES), at, w, residual, key_weight, target)
    return (update, residual[None], blended)


def solution(mesh):
    in_specs = (
        P("rep", "tp"),
        P("rep", "tp"),
        P("rep", "tp", None),
        P("tp", None),
        P("tp", None),
        P("tp", None, None),
    )
    out_specs = (P("tp", None), P("rep", "tp", None), P("tp", None))
    body = functools.partial(shards, NY, mesh.shape["rep"] // NY)
    return jax.shard_map(body, mesh=mesh, in_specs=in_specs, out_specs=out_specs, check_vma=False)
```

time: 718 us -> 75.9 us (0.11)
  the two profiles are of different devices: /device:TPU:4 before, /device:TPU:2 now
where the time goes in v1:
time: 75.9 us; the launch traced here: 75.6 us
  Pallas kernels  69.9 us (92%)
  local copies, waits for them, and re-layouts  4.95 us (7%)
    pallas_call x1, Pallas kernels, shards(): pl.pallas_call(functools.partial(first_kernel, ny, nz), out_shape=(jax.Sh...  68 us
    unnamed x14, local copies, waits for them, and re-layouts  4.95 us
    pallas_call x1, Pallas kernels, shards(): pl.pallas_call(second_kernel, out_shape=(jax.ShapeDtypeStruct((feats, wid...  1.97 us

profile of v1, /device:TPU:2, one launch (start us, length us, event | category | flops | bytes accessed | tf_op | source)
XLA Modules:
  0.0 75.6 jit_solution(10590118958175189758)
XLA Ops:
  0.6 0.0 copy-start.1
  0.6 0.0 copy-start
  0.7 0.0 copy-start.2
  0.7 1.3 %copy-done.2 = bf16[1024,512]{1,0:T(8,128)(2,1)S(1)} copy-done((bf16[1024,512]{1,0:T(8,128)(2,1)S(1)}, bf16[1024,512]{1,0:T(8,128)(2,1)}, u32[]{:S(2)}) %copy-start.2) | copy-done | bytes 1048600
  2.0 0.0 copy-start.3
  2.0 1.2 %copy-done.3 = f32[1,512,512]{2,1,0:T(8,128)S(1)} copy-done((f32[1,512,512]{2,1,0:T(8,128)S(1)}, f32[1,512,512]{2,1,0:T(8,128)}, u32[]{:S(2)}) %copy-start.3) | copy-done | bytes 1048600
  3.2 0.0 copy-start.4
  3.2 0.9 %copy-done.4 = bf16[1024,64]{0,1:T(8,128)(2,1)S(1)} copy-done((bf16[1024,64]{0,1:T(8,128)(2,1)S(1)}, bf16[1024,64]{0,1:T(8,128)(2,1)}, u32[]{:S(2)}) %copy-start.4) | copy-done | bytes 131096
  4.1 0.0 copy-start.5
  4.1 0.8 copy-done.5
  4.9 0.0 copy-start.6
  4.9 0.8 copy-done.6
  5.6 68.0 %gather_encode_sum.1 = (f32[512,512]{1,0:T(8,128)S(1)}, f32[32,1,1,128]{3,2,1,0:T(1,128)S(1)}, f32[8,64,512]{2,1,0:T(8,128)S(1)}, bf16[8,4,128,256]{3,2,1,0:T(8,128)(2,1)S(1)}) custom-call(bf16[1024,512]{1,0:T(8,128)(2,1)S(1)} %copy-done.2, bf16[64,1024]{1,0:T(8,128)(2,1)S(1)} %bitcast.6, f32[512,512]{1,0:T(8,128)S(1)} %bitcast.5, ...), custom_call_target="tpu_custom_call" | custom-call | flops 1000000000 | bytes 8000000 | tf_op jit(solution)/shard_map/gather_encode_sum/pallas_call | solution.py:326
  73.6 0.0 copy-done.1
  73.6 0.0 copy-done
  73.6 2.0 %decode_blend.1 = (f32[512,512]{1,0:T(8,128)}, f32[512,512]{1,0:T(8,128)}, bf16[512,512]{1,0:T(8,128)(2,1)}) custom-call(f32[32,1,128]{2,1,0:T(1,128)S(1)} %bitcast.4, f32[8,64,512]{2,1,0:T(8,128)S(1)} %get-tuple-element.11.at_hbm, bf16[8,4,128,256]{3,2,1,0:T(8,128)(2,1)S(1)} %get-tuple-element.12.w_hbm, f32[512,512]{1,0:T(8,128)S(1)} %get-tuple-element.13.res_in, ...), custom_call_target="tpu_custom_call" | custom-call | flops 300000000 | bytes 8000000 | tf_op jit(solution)/shard_map/decode_blend/pallas_call | solution.py:364
Async XLA Ops:
  0.6 73.0 %copy-start.1 = (bf16[512,512]{1,0:T(8,128)(2,1)S(1)}, bf16[512,512]{1,0:T(8,128)(2,1)}, u32[]{:S(2)}) copy-start(bf16[512,512]{1,0:T(8,128)(2,1)} %target_hbm.1) | copy-start | bytes 1572868
  0.6 73.0 %copy-start = (bf16[512,512]{1,0:T(8,128)(2,1)S(1)}, bf16[512,512]{1,0:T(8,128)(2,1)}, u32[]{:S(2)}) copy-start(bf16[512,512]{1,0:T(8,128)(2,1)} %weight_hbm.1) | copy-start | bytes 1572868
  0.7 1.3 %copy-start.2 = (bf16[1024,512]{1,0:T(8,128)(2,1)S(1)}, bf16[1024,512]{1,0:T(8,128)(2,1)}, u32[]{:S(2)}) copy-start(bf16[1024,512]{1,0:T(8,128)(2,1)} %tok_hbm.1) | copy-start | bytes 3145732
  2.0 1.2 %copy-start.3 = (f32[1,512,512]{2,1,0:T(8,128)S(1)}, f32[1,512,512]{2,1,0:T(8,128)}, u32[]{:S(2)}) copy-start(f32[1,512,512]{2,1,0:T(8,128)} %param.9) | copy-start | bytes 3145732
  3.2 0.9 %copy-start.4 = (bf16[1024,64]{0,1:T(8,128)(2,1)S(1)}, bf16[1024,64]{0,1:T(8,128)(2,1)}, u32[]{:S(2)}) copy-start(bf16[1024,64]{0,1:T(8,128)(2,1)} %param.8) | copy-start | bytes 393220
  4.1 0.8 %copy-start.5 = (s32[8,8,64]{2,1,0:T(8,128)S(1)}, s32[8,8,64]{2,1,0:T(8,128)}, u32[]{:S(2)}) copy-start(s32[8,8,64]{2,1,0:T(8,128)} %pos_hbm.1) | copy-start | bytes 49156
  4.9 0.8 %copy-start.6 = (bf16[128,64]{1,0:T(8,128)(2,1)S(1)}, bf16[128,64]{1,0:T(8,128)(2,1)}, u32[]{:S(2)}) copy-start(bf16[128,64]{1,0:T(8,128)(2,1)} %constant.2.clone.table_hbm) | copy-start | bytes 49156

commit v2 on v1

v2 whole, which is shorter than its diff:
```python
import functools

import jax
import jax.numpy as jnp
import ml_dtypes
import numpy as np
from jax import lax
from jax.experimental import pallas as pl
from jax.experimental.pallas import tpu as pltpu
from jax.sharding import PartitionSpec as P

BLOCK = 64
LANES = 128
NX, NY = 4, 4

momentum_decay = 0.9
polyak_rate = 0.25
update_rate = 0.1

MESH = pl.DeviceIdType.MESH
NT = (((1,), (1,)), ((), ()))


def split_table():
    index = np.arange(BLOCK, dtype=np.float64)
    angle = np.pi * (2.0 * index[:, None] + 1.0) * index[None, :] / (2.0 * BLOCK)
    scale = np.where(index == 0, np.sqrt(1.0 / BLOCK), np.sqrt(2.0 / BLOCK))
    table = np.cos(angle) * scale[None, :]
    high = table.astype(ml_dtypes.bfloat16)
    low = (table - high.astype(np.float64)).astype(ml_dtypes.bfloat16)
    return np.concatenate([high, low], axis=0)


def split_rows(value):
    high = value.astype(jnp.bfloat16)
    low = (value - high.astype(jnp.float32)).astype(jnp.bfloat16)
    return high, low


def strip_of(strip):
    return pl.ds(pl.multiple_of(strip * LANES, LANES), LANES)


def make_bases(pos_ref, table_ref, at_ref, w_ref):
    row_blocks, col_blocks, keep = pos_ref.shape
    width = col_blocks * keep
    lane = lax.broadcasted_iota(jnp.int32, (BLOCK, LANES), 1)
    level = lax.broadcasted_iota(jnp.int32, (BLOCK, width), 0)
    table = table_ref[...]
    flat = jnp.concatenate([pos_ref[:, b, :] for b in range(col_blocks)], axis=1)
    for p in range(row_blocks):
        row = flat[p : p + 1, :]
        first = jnp.where(level == (row >> 6), 1.0, 0.0).astype(jnp.bfloat16)
        second = jnp.where(level == (row & 63), 1.0, 0.0).astype(jnp.bfloat16)
        picked = jnp.dot(table, first, preferred_element_type=jnp.float32)
        at_ref[p] = picked[:BLOCK] + picked[BLOCK:]
        other = jnp.dot(table, second, preferred_element_type=jnp.float32)
        for g in range(width // LANES):
            for part in range(2):
                piece = other[part * BLOCK : (part + 1) * BLOCK, g * LANES : (g + 1) * LANES]
                top = jnp.where(lane < BLOCK, piece, 0.0).astype(jnp.bfloat16)
                low = jnp.where(lane < BLOCK, 0.0, piece).astype(jnp.bfloat16)
                w_ref[p, g, 0:BLOCK, part * LANES : (part + 1) * LANES] = top
                w_ref[p, g, BLOCK : 2 * BLOCK, part * LANES : (part + 1) * LANES] = low


def encode(block, at, w):
    high, low = split_rows(block)
    both = jnp.dot(jnp.concatenate([high, low], axis=0), w, preferred_element_type=jnp.float32)
    mixed = both[:BLOCK, :LANES] + both[:BLOCK, LANES:] + both[BLOCK:, :LANES]
    return jnp.sum(mixed * at, axis=0, keepdims=True)


def decode(values, at, w):
    high, low = split_rows(at * values)
    rows = jnp.concatenate(
        [jnp.concatenate([high, high], axis=1), jnp.concatenate([low, jnp.zeros_like(low)], axis=1)], axis=0
    )
    both = lax.dot_general(rows, w, NT, preferred_element_type=jnp.float32)
    return both[:BLOCK] + both[BLOCK:]


def first_kernel(
    ny, nz,
    tok_hbm, grad_hbm, mom_hbm, pos_hbm, table_hbm,
    res_out, total_out, at_out, w_out,
    tok, tok_t, gall, mom, at, w, pos, table, early, y_parts, z_parts, y_sums, total,
    load_sem, send_sem, recv_sem, sum_send, sum_recv, out_sem, know_y, know_z,
):
    rep, tp = lax.axis_index("rep"), lax.axis_index("tp")
    z, y = rep // ny, lax.rem(rep, ny)
    x, core = tp // 2, lax.rem(tp, 2)
    right = lax.rem(x + 1, NX) * 2 + core
    left = lax.rem(x + NX - 1, NX) * 2 + core
    far = lax.rem(x + 2, NX) * 2 + core
    other = 2 * x + 1 - core
    rows_p = at.shape[0]
    quarter = early.shape[0] // ny

    def z_peer(step):
        step = step % nz if isinstance(step, int) else step
        return {"rep": lax.rem(z + step + nz, nz) * ny + y}

    def y_peer(step):
        return {"rep": z * ny + lax.rem(y + step + ny, ny)}

    def tell(semaphore, device):
        pl.semaphore_signal(semaphore, inc=1, device_id=device, device_id_type=MESH)

    own_rows = gall.at[pl.ds(pl.multiple_of(tp * BLOCK, BLOCK), BLOCK)]
    loads = [
        pltpu.make_async_copy(pos_hbm, pos, load_sem.at[0]),
        pltpu.make_async_copy(table_hbm, table, load_sem.at[1]),
        pltpu.make_async_copy(grad_hbm, own_rows, load_sem.at[2]),
        pltpu.make_async_copy(tok_hbm, tok, load_sem.at[3]),
        pltpu.make_async_copy(mom_hbm, mom, load_sem.at[4]),
    ]

    barrier = pltpu.get_barrier_semaphore()
    for peer in (right, left, other):
        tell(barrier, {"tp": peer})
    for step in (1, -1):
        tell(barrier, z_peer(step))
        tell(barrier, y_peer(step))
    for load in loads:
        load.start()

    loads[0].wait()
    loads[1].wait()
    make_bases(pos, table, at, w)
    bases_out = [
        pltpu.make_async_copy(at, at_out, out_sem.at[0]),
        pltpu.make_async_copy(w, w_out, out_sem.at[1]),
    ]
    for copy in bases_out:
        copy.start()
    loads[2].wait()
    pl.semaphore_wait(barrier, 7)

    tell(know_y, y_peer(-1))
    tell(know_z.at[0], z_peer(1))
    tell(know_z.at[0], z_peer(-1))

    half = BLOCK // 2

    def rows(owner, part_at):
        return gall.at[pl.ds(pl.multiple_of(owner * BLOCK + part_at * half, half), half)]

    def send(number, block, device):
        copy = pltpu.make_async_remote_copy(
            src_ref=block, dst_ref=block, send_sem=send_sem.at[number], recv_sem=recv_sem.at[number],
            device_id={"tp": device}, device_id_type=MESH,
        )
        copy.start()
        return copy

    def arrived(number, block):
        pltpu.make_async_remote_copy(
            src_ref=block, dst_ref=block, send_sem=send_sem.at[number], recv_sem=recv_sem.at[number],
            device_id={"tp": other}, device_id_type=MESH,
        ).wait_recv()

    sent = [
        send(0, rows(tp, 0), right),
        send(2, rows(tp, 1), left),
        send(1, rows(tp, 1), right),
        send(3, rows(tp, 0), left),
        send(6, own_rows, other),
    ]

    loads[3].wait()
    depth = tok.shape[0]
    for at_row in range(0, depth, 256):
        tok_t[:, at_row : at_row + 256] = tok[at_row : at_row + 256, :].T
    loads[4].wait()

    pl.semaphore_wait(know_z.at[0], 2)
    tell(know_z.at[1], z_peer(2))
    tell(know_z.at[1], z_peer(-2))
    pl.semaphore_wait(know_y, 1)

    arrived(0, rows(left, 0))
    sent.append(send(4, rows(left, 0), right))
    arrived(2, rows(right, 1))
    sent.append(send(5, rows(right, 1), left))
    sent.append(send(7, rows(left, 0), other))
    sent.append(send(10, rows(right, 1), other))
    pl.semaphore_wait(know_z.at[1], 2)
    tell(know_z.at[2], z_peer(4))
    tell(know_z.at[2], z_peer(-4))
    arrived(1, rows(left, 1))
    sent.append(send(8, rows(left, 1), other))
    arrived(3, rows(right, 0))
    sent.append(send(9, rows(right, 0), other))

    def forward(strip, keep, base):
        grads = gall[pl.ds(pl.multiple_of(strip * LANES, LANES), LANES), :]
        gradient = lax.dot_general(tok_t[...], grads, NT, preferred_element_type=jnp.float32)
        moment = momentum_decay * mom[:, strip_of(strip)] + gradient
        mom[:, strip_of(strip)] = moment
        for p in range(rows_p):
            block = moment[p * BLOCK : (p + 1) * BLOCK]
            keep[base + p] = encode(block, at[p, :, strip_of(strip)], w[p, strip])

    def backward(strip, keep, base):
        for p in range(rows_p):
            field = decode(keep[base + p], at[p, :, strip_of(strip)], w[p, strip])
            mom[p * BLOCK : (p + 1) * BLOCK, strip_of(strip)] = (
                mom[p * BLOCK : (p + 1) * BLOCK, strip_of(strip)] - field
            )

    left_x, right_x, far_x = lax.rem(x + NX - 1, NX), lax.rem(x + 1, NX), lax.rem(x + 2, NX)
    left_o, right_o, far_o = left_x * 2 + 1 - core, right_x * 2 + 1 - core, far_x * 2 + 1 - core
    strips = (x, left_x, right_x, far_x)

    arrived(6, gall.at[pl.ds(pl.multiple_of(other * BLOCK, BLOCK), BLOCK)])
    forward(x, early, 0)
    arrived(7, rows(left_o, 0))
    arrived(8, rows(left_o, 1))
    forward(left_x, early, rows_p)
    pl.semaphore_wait(know_z.at[2], 2)
    tell(know_z.at[3], z_peer(8))
    tell(know_z.at[3], z_peer(-8))
    arrived(9, rows(right_o, 0))
    arrived(10, rows(right_o, 1))
    forward(right_x, early, 2 * rows_p)

    def early_y(step, carry):
        peer = lax.rem(y + step, ny)
        pltpu.make_async_remote_copy(
            src_ref=early.at[pl.ds(peer * quarter, quarter)], dst_ref=y_parts.at[y],
            send_sem=sum_send.at[0], recv_sem=sum_recv.at[0], device_id=y_peer(step), device_id_type=MESH,
        ).start()
        return carry

    lax.fori_loop(1, ny, early_y, 0)
    y_parts[y] = early[pl.ds(y * quarter, quarter)]

    arrived(4, rows(far, 0))
    sent.append(send(11, rows(far, 0), other))
    arrived(5, rows(far, 1))
    sent.append(send(12, rows(far, 1), other))
    arrived(11, rows(far_o, 0))
    arrived(12, rows(far_o, 1))
    mine = z_parts.at[z]
    forward(far_x, mine, quarter)

    three = y_parts.at[pl.ds(0, ny - 1)]
    pltpu.make_async_copy(three, three, sum_recv.at[0]).wait()
    mine[0:quarter] = jnp.sum(y_parts[...], axis=0)
    pl.semaphore_wait(know_z.at[3], 2)

    def across(step):
        pltpu.make_async_remote_copy(
            src_ref=mine, dst_ref=mine, send_sem=sum_send.at[1], recv_sem=sum_recv.at[1],
            device_id=z_peer(step), device_id_type=MESH,
        ).start()

    def both_ways(step, carry):
        across(nz // 2 - step)
        across(step - nz // 2)
        return carry

    across(nz // 2)
    lax.fori_loop(1, nz // 2, both_ways, 0)
    for number, strip in enumerate(strips[:3]):
        backward(strip, early, number * rows_p)
    backward(far_x, mine, quarter)
    res_copy = pltpu.make_async_copy(mom, res_out, out_sem.at[2])
    res_copy.start()
    many = z_parts.at[pl.ds(0, nz - 1)]
    pltpu.make_async_copy(many, many, sum_recv.at[1]).wait()
    y_sums[y] = jnp.sum(z_parts[...], axis=0)

    def late_y(step, carry):
        pltpu.make_async_remote_copy(
            src_ref=y_sums.at[y], dst_ref=y_sums.at[y], send_sem=sum_send.at[2], recv_sem=sum_recv.at[2],
            device_id=y_peer(step), device_id_type=MESH,
        ).start()
        return carry

    lax.fori_loop(1, ny, late_y, 0)
    some = y_sums.at[pl.ds(0, ny - 1)]
    pltpu.make_async_copy(some, some, sum_recv.at[2]).wait()
    for number, strip in enumerate(strips[:3]):
        for p in range(rows_p):
            row = number * rows_p + p
            total[strip * rows_p + p] = y_sums[row // quarter, row % quarter]
    last = jnp.sum(y_sums[:, quarter:], axis=0)
    for p in range(rows_p):
        total[far_x * rows_p + p] = last[p]
    total_copy = pltpu.make_async_copy(total, total_out, out_sem.at[3])
    total_copy.start()

    for copy in sent:
        copy.wait_send()
    pltpu.make_async_copy(three, three, sum_send.at[0]).wait()
    pltpu.make_async_copy(many, many, sum_send.at[1]).wait()
    pltpu.make_async_copy(some, some, sum_send.at[2]).wait()
    for copy in bases_out:
        copy.wait()
    res_copy.wait()
    total_copy.wait()


def second_kernel(
    total, at, w, res_in, weight, target,
    update_hbm, res_hbm, blended_hbm,
    update, blended, out_sem,
):
    res_copy = pltpu.make_async_copy(res_in, res_hbm, out_sem.at[0])
    res_copy.start()
    rows_p, strips = w.shape[:2]
    outs = []
    for p in range(rows_p):
        at_rows = slice(p * BLOCK, (p + 1) * BLOCK)
        for g in range(strips):
            at_lanes = slice(g * LANES, (g + 1) * LANES)
            field = decode(total[g * rows_p + p], at[p, :, at_lanes], w[p, g])
            update[at_rows, at_lanes] = field
            moved = weight[at_rows, at_lanes].astype(jnp.float32) - update_rate * field
            mixed = (1.0 - polyak_rate) * target[at_rows, at_lanes].astype(jnp.float32) + polyak_rate * moved
            blended[at_rows, at_lanes] = mixed.astype(jnp.bfloat16)
        outs.append(pltpu.make_async_copy(update.at[at_rows], update_hbm.at[at_rows], out_sem.at[1 + 2 * p]))
        outs.append(pltpu.make_async_copy(blended.at[at_rows], blended_hbm.at[at_rows], out_sem.at[2 + 2 * p]))
        outs[-2].start()
        outs[-1].start()
    for copy in outs:
        copy.wait()
    res_copy.wait()


def shards(ny, nz, tokens, key_grad, momentum, key_weight, target, positions):
    anywhere = pl.BlockSpec(memory_space=pl.ANY)
    table = jnp.asarray(split_table())
    depth, feats = tokens.shape
    _, _, width = momentum.shape
    rows_p, col_blocks, keep = positions.shape
    strips = width // LANES
    rows = rows_p * strips
    at_shape, w_shape = (rows_p, BLOCK, width), (rows_p, strips, 2 * BLOCK, 2 * LANES)
    early = (strips - 1) * rows_p
    quarter = early // ny
    residual, total, at, w = pl.pallas_call(
        functools.partial(first_kernel, ny, nz),
        out_shape=(
            pltpu.VMEM((feats, width), jnp.float32),
            pltpu.VMEM((rows, 1, LANES), jnp.float32),
            pltpu.VMEM(at_shape, jnp.float32),
            pltpu.VMEM(w_shape, jnp.bfloat16),
        ),
        in_specs=[anywhere] * 5,
        out_specs=(anywhere,) * 4,
        scratch_shapes=[
            pltpu.VMEM((depth, feats), jnp.bfloat16),
            pltpu.VMEM((feats, depth), jnp.bfloat16),
            pltpu.VMEM((width, depth), jnp.bfloat16),
            pltpu.VMEM((feats, width), jnp.float32),
            pltpu.VMEM(at_shape, jnp.float32),
            pltpu.VMEM(w_shape, jnp.bfloat16),
            pltpu.VMEM((rows_p, col_blocks, keep), jnp.int32),
            pltpu.VMEM(table.shape, jnp.bfloat16),
            pltpu.VMEM((early, 1, LANES), jnp.float32),
            pltpu.VMEM((ny, quarter, 1, LANES), jnp.float32),
            pltpu.VMEM((nz, quarter + rows_p, 1, LANES), jnp.float32),
            pltpu.VMEM((ny, quarter + rows_p, 1, LANES), jnp.float32),
            pltpu.VMEM((rows, 1, LANES), jnp.float32),
            pltpu.SemaphoreType.DMA((5,)),
            pltpu.SemaphoreType.DMA((13,)),
            pltpu.SemaphoreType.DMA((13,)),
            pltpu.SemaphoreType.DMA((3,)),
            pltpu.SemaphoreType.DMA((3,)),
            pltpu.SemaphoreType.DMA((4,)),
            pltpu.SemaphoreType.REGULAR,
            pltpu.SemaphoreType.REGULAR((4,)),
        ],
        compiler_params=pltpu.CompilerParams(
            collective_id=0, has_side_effects=True, vmem_limit_bytes=54 * 1024 * 1024
        ),
        cost_estimate=pl.CostEstimate(flops=1_000_000_000, bytes_accessed=8_000_000, transcendentals=0),
        name="gather_encode_sum",
    )(tokens, key_grad.T, momentum[0], positions, table)
    in_vmem = pl.BlockSpec(memory_space=pltpu.VMEM)
    update, residual, blended = pl.pallas_call(
        second_kernel,
        out_shape=(
            jax.ShapeDtypeStruct((feats, width), jnp.float32),
            jax.ShapeDtypeStruct((feats, width), jnp.float32),
            jax.ShapeDtypeStruct((feats, width), jnp.bfloat16),
        ),
        in_specs=[in_vmem] * 3 + [anywhere] + [in_vmem] * 2,
        out_specs=(anywhere,) * 3,
        scratch_shapes=[
            pltpu.VMEM((feats, width), jnp.float32),
            pltpu.VMEM((feats, width), jnp.bfloat16),
            pltpu.SemaphoreType.DMA((1 + 2 * rows_p,)),
        ],
        compiler_params=pltpu.CompilerParams(vmem_limit_bytes=32 * 1024 * 1024),
        cost_estimate=pl.CostEstimate(flops=300_000_000, bytes_accessed=8_000_000, transcendentals=0),
        name="decode_blend",
    )(total, at, w, residual, key_weight, target)
    return (update, residual[None], blended)


def solution(mesh):
    in_specs = (
        P("rep", "tp"),
        P("rep", "tp"),
        P("rep", "tp", None),
        P("tp", None),
        P("tp", None),
        P("tp", None, None),
    )
    out_specs = (P("tp", None), P("rep", "tp", None), P("tp", None))
    body = functools.partial(shards, NY, mesh.shape["rep"] // NY)
    return jax.shard_map(body, mesh=mesh, in_specs=in_specs, out_specs=out_specs, check_vma=False)
```

time: 75.9 us -> 63.8 us (0.84)
  the two profiles are of different devices: /device:TPU:2 before, /device:TPU:32 now
where the time goes in v2:
time: 63.8 us; the launch traced here: 63.6 us
  Pallas kernels  62.9 us (99%)
  between operations  0.67 us (1%)
    pallas_call x1, Pallas kernels, shards(): pl.pallas_call(functools.partial(first_kernel, ny, nz), out_shape=(pltpu....  61.3 us
    pallas_call x1, Pallas kernels, shards(): pl.pallas_call(second_kernel, out_shape=(jax.ShapeDtypeStruct((feats, wid...  1.63 us

profile of v2, /device:TPU:32, one launch (start us, length us, event | category | flops | bytes accessed | tf_op | source)
XLA Modules:
  0.0 63.6 jit_solution(1195739395418587604)
XLA Ops:
  0.6 0.0 copy-start.1
  0.6 0.0 copy-start
  0.7 61.3 %gather_encode_sum.1 = (f32[512,512]{1,0:T(8,128)S(1)}, f32[32,1,128]{2,1,0:T(1,128)S(1)}, f32[8,64,512]{2,1,0:T(8,128)S(1)}, bf16[8,4,128,256]{3,2,1,0:T(8,128)(2,1)S(1)}) custom-call(bf16[1024,512]{1,0:T(8,128)(2,1)} %tok_hbm.1, bf16[64,1024]{1,0:T(8,128)(2,1)} %bitcast.5, f32[512,512]{1,0:T(8,128)} %bitcast.3, s32[8,8,64]{2,1,0:T(8,128)} %pos_hbm.1, ...), custom_call_target="tpu_custom_call" | custom-call | flops 1000000000 | bytes 8000000 | tf_op jit(solution)/shard_map/gather_encode_sum/pallas_call | solution.py:344
  62.0 0.0 copy-done.1
  62.0 0.0 copy-done
  62.0 1.6 %decode_blend.1 = (f32[512,512]{1,0:T(8,128)}, f32[512,512]{1,0:T(8,128)}, bf16[512,512]{1,0:T(8,128)(2,1)}) custom-call(f32[32,1,128]{2,1,0:T(1,128)S(1)} %get-tuple-element.10.total, f32[8,64,512]{2,1,0:T(8,128)S(1)} %get-tuple-element.11.at, bf16[8,4,128,256]{3,2,1,0:T(8,128)(2,1)S(1)} %get-tuple-element.12.w, f32[512,512]{1,0:T(8,128)S(1)} %get-tuple-element.13.res_in, ...), custom_call_target="tpu_custom_call" | custom-call | flops 300000000 | bytes 8000000 | tf_op jit(solution)/shard_map/decode_blend/pallas_call | solution.py:384
Async XLA Ops:
  0.6 61.3 %copy-start.1 = (bf16[512,512]{1,0:T(8,128)(2,1)S(1)}, bf16[512,512]{1,0:T(8,128)(2,1)}, u32[]{:S(2)}) copy-start(bf16[512,512]{1,0:T(8,128)(2,1)} %target.1) | copy-start | bytes 1572868
  0.6 61.3 %copy-start = (bf16[512,512]{1,0:T(8,128)(2,1)S(1)}, bf16[512,512]{1,0:T(8,128)(2,1)}, u32[]{:S(2)}) copy-start(bf16[512,512]{1,0:T(8,128)(2,1)} %weight.1) | copy-start | bytes 1572868

commit v3 on v2

--- a/solution.py
+++ b/solution.py
@@ -84,8 +84,8 @@
     ny, nz,
     tok_hbm, grad_hbm, mom_hbm, pos_hbm, table_hbm,
     res_out, total_out, at_out, w_out,
-    tok, tok_t, gall, mom, at, w, pos, table, early, y_parts, z_parts, y_sums, total,
-    load_sem, send_sem, recv_sem, sum_send, sum_recv, out_sem, know_y, know_z,
+    tok, tok_t, gall, mom, at, w, pos, table, early, late, y_parts, z_parts, y_sums, total,
+    load_sem, send_sem, recv_sem, sum_send, sum_recv, out_sem, know_y, know_down, know_up,
 ):
     rep, tp = lax.axis_index("rep"), lax.axis_index("tp")
     z, y = rep // ny, lax.rem(rep, ny)
@@ -116,15 +116,67 @@
         pltpu.make_async_copy(mom_hbm, mom, load_sem.at[4]),
     ]
 
+    loads[2].start()
     barrier = pltpu.get_barrier_semaphore()
     for peer in (right, left, other):
         tell(barrier, {"tp": peer})
     for step in (1, -1):
         tell(barrier, z_peer(step))
         tell(barrier, y_peer(step))
-    for load in loads:
-        load.start()
-
+    for number in (3, 4, 0, 1):
+        loads[number].start()
+
+    loads[2].wait()
+    pl.semaphore_wait(barrier, 7)
+
+    half = BLOCK // 2
+
+    def rows(owner, part_at):
+        return gall.at[pl.ds(pl.multiple_of(owner * BLOCK + part_at * half, half), half)]
+
+    def send(number, block, device):
+        copy = pltpu.make_async_remote_copy(
+            src_ref=block, dst_ref=block, send_sem=send_sem.at[number], recv_sem=recv_sem.at[number],
+            device_id={"tp": device}, device_id_type=MESH,
+        )
+        copy.start()
+        return copy
+
+    def arrived(number, block):
+        pltpu.make_async_remote_copy(
+            src_ref=block, dst_ref=block, send_sem=send_sem.at[number], recv_sem=recv_sem.at[number],
+            device_id={"tp": other}, device_id_type=MESH,
+        ).wait_recv()
+
+    sent = [
+        send(0, rows(tp, 0), right),
+        send(2, rows(tp, 1), left),
+        send(1, rows(tp, 1), right),
+        send(3, rows(tp, 0), left),
+        send(6, own_rows, other),
+    ]
+
+    def pass_on(level):
+        tell(know_down.at[level], z_peer(1 << level))
+        tell(know_up.at[level], z_peer(-(1 << level)))
+
+    def learn(level):
+        pl.semaphore_wait(know_down.at[level], 1)
+        pl.semaphore_wait(know_up.at[level], 1)
+        if level + 1 < levels:
+            pass_on(level + 1)
+
+    levels = know_down.shape[0]
+    tell(know_y, y_peer(-1))
+    pass_on(0)
+
+    loads[3].wait()
+    depth = tok.shape[0]
+    for at_row in range(0, depth, 256):
+        tok_t[:, at_row : at_row + 256] = tok[at_row : at_row + 256, :].T
+    loads[4].wait()
+    pl.semaphore_wait(know_y, 1)
+    learn(0)
     loads[0].wait()
     loads[1].wait()
     make_bases(pos, table, at, w)
@@ -134,50 +186,7 @@
     ]
     for copy in bases_out:
         copy.start()
-    loads[2].wait()
-    pl.semaphore_wait(barrier, 7)
-
-    tell(know_y, y_peer(-1))
-    tell(know_z.at[0], z_peer(1))
-    tell(know_z.at[0], z_peer(-1))
-
-    half = BLOCK // 2
-
-    def rows(owner, part_at):
-        return gall.at[pl.ds(pl.multiple_of(owner * BLOCK + part_at * half, half), half)]
-
-    def send(number, block, device):
-        copy = pltpu.make_async_remote_copy(
-            src_ref=block, dst_ref=block, send_sem=send_sem.at[number], recv_sem=recv_sem.at[number],
-            device_id={"tp": device}, device_id_type=MESH,
-        )
-        copy.start()
-        return copy
-
-    def arrived(number, block):
-        pltpu.make_async_remote_copy(
-            src_ref=block, dst_ref=block, send_sem=send_sem.at[number], recv_sem=recv_sem.at[number],
-            device_id={"tp": other}, device_id_type=MESH,
-        ).wait_recv()
-
-    sent = [
-        send(0, rows(tp, 0), right),
-        send(2, rows(tp, 1), left),
-        send(1, rows(tp, 1), right),
-        send(3, rows(tp, 0), left),
-        send(6, own_rows, other),
-    ]
-
-    loads[3].wait()
-    depth = tok.shape[0]
-    for at_row in range(0, depth, 256):
-        tok_t[:, at_row : at_row + 256] = tok[at_row : at_row + 256, :].T
-    loads[4].wait()
-
-    pl.semaphore_wait(know_z.at[0], 2)
-    tell(know_z.at[1], z_peer(2))
-    tell(know_z.at[1], z_peer(-2))
-    pl.semaphore_wait(know_y, 1)
+    learn(1)
 
     arrived(0, rows(left, 0))
     sent.append(send(4, rows(left, 0), right))
@@ -185,9 +194,6 @@
     sent.append(send(5, rows(right, 1), left))
     sent.append(send(7, rows(left, 0), other))
     sent.append(send(10, rows(right, 1), other))
-    pl.semaphore_wait(know_z.at[1], 2)
-    tell(know_z.at[2], z_peer(4))
-    tell(know_z.at[2], z_peer(-4))
     arrived(1, rows(left, 1))
     sent.append(send(8, rows(left, 1), other))
     arrived(3, rows(right, 0))
@@ -218,9 +224,8 @@
     arrived(7, rows(left_o, 0))
     arrived(8, rows(left_o, 1))
     forward(left_x, early, rows_p)
-    pl.semaphore_wait(know_z.at[2], 2)
-    tell(know_z.at[3], z_peer(8))
-    tell(know_z.at[3], z_peer(-8))
+    for level in range(2, levels - 1):
+        learn(level)
     arrived(9, rows(right_o, 0))
     arrived(10, rows(right_o, 1))
     forward(right_x, early, 2 * rows_p)
@@ -242,17 +247,19 @@
     sent.append(send(12, rows(far, 1), other))
     arrived(11, rows(far_o, 0))
     arrived(12, rows(far_o, 1))
-    mine = z_parts.at[z]
-    forward(far_x, mine, quarter)
+    forward(far_x, late, 0)
 
     three = y_parts.at[pl.ds(0, ny - 1)]
     pltpu.make_async_copy(three, three, sum_recv.at[0]).wait()
-    mine[0:quarter] = jnp.sum(y_parts[...], axis=0)
-    pl.semaphore_wait(know_z.at[3], 2)
+    firsts = jnp.sum(y_parts[...], axis=0)
+    rest = jnp.zeros((z_parts.shape[1] - quarter - rows_p, LANES), jnp.float32)
+    mine = [firsts[row] for row in range(quarter)] + [late[p] for p in range(rows_p)] + [rest]
+    z_parts[z] = jnp.concatenate(mine, axis=0).astype(jnp.bfloat16)
+    learn(levels - 1)
 
     def across(step):
         pltpu.make_async_remote_copy(
-            src_ref=mine, dst_ref=mine, send_sem=sum_send.at[1], recv_sem=sum_recv.at[1],
+            src_ref=z_parts.at[z], dst_ref=z_parts.at[z], send_sem=sum_send.at[1], recv_sem=sum_recv.at[1],
             device_id=z_peer(step), device_id_type=MESH,
         ).start()
 
@@ -265,12 +272,12 @@
     lax.fori_loop(1, nz // 2, both_ways, 0)
     for number, strip in enumerate(strips[:3]):
         backward(strip, early, number * rows_p)
-    backward(far_x, mine, quarter)
+    backward(far_x, late, 0)
     res_copy = pltpu.make_async_copy(mom, res_out, out_sem.at[2])
     res_copy.start()
     many = z_parts.at[pl.ds(0, nz - 1)]
     pltpu.make_async_copy(many, many, sum_recv.at[1]).wait()
-    y_sums[y] = jnp.sum(z_parts[...], axis=0)
+    y_sums[y] = jnp.sum(z_parts[...].astype(jnp.float32), axis=0)
 
     def late_y(step, carry):
         pltpu.make_async_remote_copy(
@@ -285,10 +292,11 @@
     for number, strip in enumerate(strips[:3]):
         for p in range(rows_p):
             row = number * rows_p + p
-            total[strip * rows_p + p] = y_sums[row // quarter, row % quarter]
-    last = jnp.sum(y_sums[:, quarter:], axis=0)
+            at_row = row % quarter
+            total[strip * rows_p + p] = y_sums[row // quarter, at_row : at_row + 1]
+    last = jnp.sum(y_sums[...], axis=0)
     for p in range(rows_p):
-        total[far_x * rows_p + p] = last[p]
+        total[far_x * rows_p + p] = last[quarter + p : quarter + p + 1]
     total_copy = pltpu.make_async_copy(total, total_out, out_sem.at[3])
     total_copy.start()
 
@@ -361,9 +369,10 @@
             pltpu.VMEM((rows_p, col_blocks, keep), jnp.int32),
             pltpu.VMEM(table.shape, jnp.bfloat16),
             pltpu.VMEM((early, 1, LANES), jnp.float32),
+            pltpu.VMEM((rows_p, 1, LANES), jnp.float32),
             pltpu.VMEM((ny, quarter, 1, LANES), jnp.float32),
-            pltpu.VMEM((nz, quarter + rows_p, 1, LANES), jnp.float32),
-            pltpu.VMEM((ny, quarter + rows_p, 1, LANES), jnp.float32),
+            pltpu.VMEM((nz, 16, LANES), jnp.bfloat16),
+            pltpu.VMEM((ny, 16, LANES), jnp.float32),
             pltpu.VMEM((rows, 1, LANES), jnp.float32),
             pltpu.SemaphoreType.DMA((5,)),
             pltpu.SemaphoreType.DMA((13,)),
@@ -372,7 +381,8 @@
             pltpu.SemaphoreType.DMA((3,)),
             pltpu.SemaphoreType.DMA((4,)),
             pltpu.SemaphoreType.REGULAR,
-            pltpu.SemaphoreType.REGULAR((4,)),
+            pltpu.SemaphoreType.REGULAR(((nz // 2).bit_length() - 1,)),
+            pltpu.SemaphoreType.REGULAR(((nz // 2).bit_length() - 1,)),
         ],
         compiler_params=pltpu.CompilerParams(
             collective_id=0, has_side_effects=True, vmem_limit_bytes=54 * 1024 * 1024

time: 63.8 us -> 55.3 us (0.87)
  the two profiles are of different devices: /device:TPU:32 before, /device:TPU:2 now
where the time goes in v3:
time: 55.3 us; the launch traced here: 55.2 us
  Pallas kernels  54.5 us (99%)
  between operations  0.67 us (1%)
    pallas_call x1, Pallas kernels, shards(): pl.pallas_call(functools.partial(first_kernel, ny, nz), out_shape=(pltpu....  52.9 us
    pallas_call x1, Pallas kernels, shards(): pl.pallas_call(second_kernel, out_shape=(jax.ShapeDtypeStruct((feats, wid...  1.63 us

profile of v3, /device:TPU:2, one launch (start us, length us, event | category | flops | bytes accessed | tf_op | source)
XLA Modules:
  0.0 55.2 jit_solution(4196949572559452373)
XLA Ops:
  0.6 0.0 copy-start.1
  0.6 0.0 copy-start
  0.7 52.9 %gather_encode_sum.1 = (f32[512,512]{1,0:T(8,128)S(1)}, f32[32,1,128]{2,1,0:T(1,128)S(1)}, f32[8,64,512]{2,1,0:T(8,128)S(1)}, bf16[8,4,128,256]{3,2,1,0:T(8,128)(2,1)S(1)}) custom-call(bf16[1024,512]{1,0:T(8,128)(2,1)} %tok_hbm.1, bf16[64,1024]{1,0:T(8,128)(2,1)} %bitcast.5, f32[512,512]{1,0:T(8,128)} %bitcast.3, s32[8,8,64]{2,1,0:T(8,128)} %pos_hbm.1, ...), custom_call_target="tpu_custom_call" | custom-call | flops 1000000000 | bytes 8000000 | tf_op jit(solution)/shard_map/gather_encode_sum/pallas_call | solution.py:352
  53.5 0.0 copy-done.1
  53.6 0.0 copy-done
  53.6 1.6 %decode_blend.1 = (f32[512,512]{1,0:T(8,128)}, f32[512,512]{1,0:T(8,128)}, bf16[512,512]{1,0:T(8,128)(2,1)}) custom-call(f32[32,1,128]{2,1,0:T(1,128)S(1)} %get-tuple-element.10.total, f32[8,64,512]{2,1,0:T(8,128)S(1)} %get-tuple-element.11.at, bf16[8,4,128,256]{3,2,1,0:T(8,128)(2,1)S(1)} %get-tuple-element.12.w, f32[512,512]{1,0:T(8,128)S(1)} %get-tuple-element.13.res_in, ...), custom_call_target="tpu_custom_call" | custom-call | flops 300000000 | bytes 8000000 | tf_op jit(solution)/shard_map/decode_blend/pallas_call | solution.py:394
Async XLA Ops:
  0.6 52.9 %copy-start.1 = (bf16[512,512]{1,0:T(8,128)(2,1)S(1)}, bf16[512,512]{1,0:T(8,128)(2,1)}, u32[]{:S(2)}) copy-start(bf16[512,512]{1,0:T(8,128)(2,1)} %target.1) | copy-start | bytes 1572868
  0.6 52.9 %copy-start = (bf16[512,512]{1,0:T(8,128)(2,1)S(1)}, bf16[512,512]{1,0:T(8,128)(2,1)}, u32[]{:S(2)}) copy-start(bf16[512,512]{1,0:T(8,128)(2,1)} %weight.1) | copy-start | bytes 1572868

commit v4 on v3

--- a/solution.py
+++ b/solution.py
@@ -85,7 +85,7 @@
     tok_hbm, grad_hbm, mom_hbm, pos_hbm, table_hbm,
     res_out, total_out, at_out, w_out,
     tok, tok_t, gall, mom, at, w, pos, table, early, late, y_parts, z_parts, y_sums, total,
-    load_sem, send_sem, recv_sem, sum_send, sum_recv, out_sem, know_y, know_down, know_up,
+    load_sem, send_sem, recv_sem, sum_send, sum_recv, out_sem, know_down, know_up,
 ):
     rep, tp = lax.axis_index("rep"), lax.axis_index("tp")
     z, y = rep // ny, lax.rem(rep, ny)
@@ -120,15 +120,29 @@
     barrier = pltpu.get_barrier_semaphore()
     for peer in (right, left, other):
         tell(barrier, {"tp": peer})
-    for step in (1, -1):
+    for step in (2, -2, 1, -1):
         tell(barrier, z_peer(step))
+    for step in range(1, ny):
         tell(barrier, y_peer(step))
     for number in (3, 4, 0, 1):
         loads[number].start()
 
     loads[2].wait()
-    pl.semaphore_wait(barrier, 7)
-
+    pl.semaphore_wait(barrier, 3 + 4 + ny - 1)
+
+    levels = know_down.shape[0]
+
+    def pass_on(level):
+        tell(know_down.at[level], z_peer(2 << level))
+        tell(know_up.at[level], z_peer(-(2 << level)))
+
+    def learn(level):
+        pl.semaphore_wait(know_down.at[level], 1)
+        pl.semaphore_wait(know_up.at[level], 1)
+        if level + 1 < levels:
+            pass_on(level + 1)
+
+    pass_on(0)
     half = BLOCK // 2
 
     def rows(owner, part_at):
@@ -156,27 +170,11 @@
         send(6, own_rows, other),
     ]
 
-    def pass_on(level):
-        tell(know_down.at[level], z_peer(1 << level))
-        tell(know_up.at[level], z_peer(-(1 << level)))
-
-    def learn(level):
-        pl.semaphore_wait(know_down.at[level], 1)
-        pl.semaphore_wait(know_up.at[level], 1)
-        if level + 1 < levels:
-            pass_on(level + 1)
-
-    levels = know_down.shape[0]
-    tell(know_y, y_peer(-1))
-    pass_on(0)
-
     loads[3].wait()
     depth = tok.shape[0]
     for at_row in range(0, depth, 256):
         tok_t[:, at_row : at_row + 256] = tok[at_row : at_row + 256, :].T
     loads[4].wait()
-    pl.semaphore_wait(know_y, 1)
-    learn(0)
     loads[0].wait()
     loads[1].wait()
     make_bases(pos, table, at, w)
@@ -186,7 +184,7 @@
     ]
     for copy in bases_out:
         copy.start()
-    learn(1)
+    learn(0)
 
     arrived(0, rows(left, 0))
     sent.append(send(4, rows(left, 0), right))
@@ -221,11 +219,11 @@
 
     arrived(6, gall.at[pl.ds(pl.multiple_of(other * BLOCK, BLOCK), BLOCK)])
     forward(x, early, 0)
+    for level in range(1, levels - 1):
+        learn(level)
     arrived(7, rows(left_o, 0))
     arrived(8, rows(left_o, 1))
     forward(left_x, early, rows_p)
-    for level in range(2, levels - 1):
-        learn(level)
     arrived(9, rows(right_o, 0))
     arrived(10, rows(right_o, 1))
     forward(right_x, early, 2 * rows_p)
@@ -380,9 +378,8 @@
             pltpu.SemaphoreType.DMA((3,)),
             pltpu.SemaphoreType.DMA((3,)),
             pltpu.SemaphoreType.DMA((4,)),
-            pltpu.SemaphoreType.REGULAR,
-            pltpu.SemaphoreType.REGULAR(((nz // 2).bit_length() - 1,)),
-            pltpu.SemaphoreType.REGULAR(((nz // 2).bit_length() - 1,)),
+            pltpu.SemaphoreType.REGULAR(((nz // 2).bit_length() - 2,)),
+            pltpu.SemaphoreType.REGULAR(((nz // 2).bit_length() - 2,)),
         ],
         compiler_params=pltpu.CompilerParams(
             collective_id=0, has_side_effects=True, vmem_limit_bytes=54 * 1024 * 1024

time: 55.3 us -> 53.9 us (0.975)
  Pallas kernels: 54.5 us -> 53.1 us
    pallas_call x1, Pallas kernels: 52.9 us -> 51.5 us  [shards(): pl.pallas_call(functools.partial(first_kernel, ny, nz), out_shape=(pltpu....]
where the time goes in v4:
time: 53.9 us; the launch traced here: 53.8 us
  Pallas kernels  53.1 us (99%)
  between operations  0.67 us (1%)
    pallas_call x1, Pallas kernels, shards(): pl.pallas_call(functools.partial(first_kernel, ny, nz), out_shape=(pltpu....  51.5 us
    pallas_call x1, Pallas kernels, shards(): pl.pallas_call(second_kernel, out_shape=(jax.ShapeDtypeStruct((feats, wid...  1.63 us

profile of v4, /device:TPU:2, one launch (start us, length us, event | category | flops | bytes accessed | tf_op | source)
XLA Modules:
  0.0 53.8 jit_solution(8731427714781186401)
XLA Ops:
  0.6 0.0 copy-start.1
  0.6 0.0 copy-start
  0.7 51.5 %gather_encode_sum.1 = (f32[512,512]{1,0:T(8,128)S(1)}, f32[32,1,128]{2,1,0:T(1,128)S(1)}, f32[8,64,512]{2,1,0:T(8,128)S(1)}, bf16[8,4,128,256]{3,2,1,0:T(8,128)(2,1)S(1)}) custom-call(bf16[1024,512]{1,0:T(8,128)(2,1)} %tok_hbm.1, bf16[64,1024]{1,0:T(8,128)(2,1)} %bitcast.5, f32[512,512]{1,0:T(8,128)} %bitcast.3, s32[8,8,64]{2,1,0:T(8,128)} %pos_hbm.1, ...), custom_call_target="tpu_custom_call" | custom-call | flops 1000000000 | bytes 8000000 | tf_op jit(solution)/shard_map/gather_encode_sum/pallas_call | solution.py:350
  52.1 0.0 copy-done.1
  52.1 0.0 copy-done
  52.1 1.6 %decode_blend.1 = (f32[512,512]{1,0:T(8,128)}, f32[512,512]{1,0:T(8,128)}, bf16[512,512]{1,0:T(8,128)(2,1)}) custom-call(f32[32,1,128]{2,1,0:T(1,128)S(1)} %get-tuple-element.10.total, f32[8,64,512]{2,1,0:T(8,128)S(1)} %get-tuple-element.11.at, bf16[8,4,128,256]{3,2,1,0:T(8,128)(2,1)S(1)} %get-tuple-element.12.w, f32[512,512]{1,0:T(8,128)S(1)} %get-tuple-element.13.res_in, ...), custom_call_target="tpu_custom_call" | custom-call | flops 300000000 | bytes 8000000 | tf_op jit(solution)/shard_map/decode_blend/pallas_call | solution.py:391
Async XLA Ops:
  0.6 51.5 %copy-start.1 = (bf16[512,512]{1,0:T(8,128)(2,1)S(1)}, bf16[512,512]{1,0:T(8,128)(2,1)}, u32[]{:S(2)}) copy-start(bf16[512,512]{1,0:T(8,128)(2,1)} %target.1) | copy-start | bytes 1572868
  0.6 51.5 %copy-start = (bf16[512,512]{1,0:T(8,128)(2,1)S(1)}, bf16[512,512]{1,0:T(8,128)(2,1)}, u32[]{:S(2)}) copy-start(bf16[512,512]{1,0:T(8,128)(2,1)} %weight.1) | copy-start | bytes 1572868

commit v5 on v4

--- a/solution.py
+++ b/solution.py
@@ -84,7 +84,7 @@
     ny, nz,
     tok_hbm, grad_hbm, mom_hbm, pos_hbm, table_hbm,
     res_out, total_out, at_out, w_out,
-    tok, tok_t, gall, mom, at, w, pos, table, early, late, y_parts, z_parts, y_sums, total,
+    tok, tok_t, gall, mom, at, w, pos, table, early, late, y_parts, y_lasts, z_parts, y_sums, total,
     load_sem, send_sem, recv_sem, sum_send, sum_recv, out_sem, know_down, know_up,
 ):
     rep, tp = lax.axis_index("rep"), lax.axis_index("tp")
@@ -95,7 +95,7 @@
     far = lax.rem(x + 2, NX) * 2 + core
     other = 2 * x + 1 - core
     rows_p = at.shape[0]
-    quarter = early.shape[0] // ny
+    quarter, share = early.shape[0] // ny, rows_p // ny
 
     def z_peer(step):
         step = step % nz if isinstance(step, int) else step
@@ -247,11 +247,26 @@
     arrived(12, rows(far_o, 1))
     forward(far_x, late, 0)
 
+    def last_y(step, carry):
+        peer = lax.rem(y + step, ny)
+        pltpu.make_async_remote_copy(
+            src_ref=late.at[pl.ds(peer * share, share)], dst_ref=y_lasts.at[y],
+            send_sem=sum_send.at[3], recv_sem=sum_recv.at[3], device_id=y_peer(step), device_id_type=MESH,
+        ).start()
+        return carry
+
+    lax.fori_loop(1, ny, last_y, 0)
+    y_lasts[y] = late[pl.ds(y * share, share)]
+    for number, strip in enumerate(strips[:3]):
+        backward(strip, early, number * rows_p)
+
     three = y_parts.at[pl.ds(0, ny - 1)]
     pltpu.make_async_copy(three, three, sum_recv.at[0]).wait()
     firsts = jnp.sum(y_parts[...], axis=0)
-    rest = jnp.zeros((z_parts.shape[1] - quarter - rows_p, LANES), jnp.float32)
-    mine = [firsts[row] for row in range(quarter)] + [late[p] for p in range(rows_p)] + [rest]
+    others = y_lasts.at[pl.ds(0, ny - 1)]
+    pltpu.make_async_copy(others, others, sum_recv.at[3]).wait()
+    lasts = jnp.sum(y_lasts[...], axis=0)
+    mine = [firsts[row] for row in range(quarter)] + [lasts[row] for row in range(share)]
     z_parts[z] = jnp.concatenate(mine, axis=0).astype(jnp.bfloat16)
     learn(levels - 1)
 
@@ -268,8 +283,6 @@
 
     across(nz // 2)
     lax.fori_loop(1, nz // 2, both_ways, 0)
-    for number, strip in enumerate(strips[:3]):
-        backward(strip, early, number * rows_p)
     backward(far_x, late, 0)
     res_copy = pltpu.make_async_copy(mom, res_out, out_sem.at[2])
     res_copy.start()
@@ -292,15 +305,16 @@
             row = number * rows_p + p
             at_row = row % quarter
             total[strip * rows_p + p] = y_sums[row // quarter, at_row : at_row + 1]
-    last = jnp.sum(y_sums[...], axis=0)
     for p in range(rows_p):
-        total[far_x * rows_p + p] = last[quarter + p : quarter + p + 1]
+        at_row = quarter + p % share
+        total[far_x * rows_p + p] = y_sums[p // share, at_row : at_row + 1]
     total_copy = pltpu.make_async_copy(total, total_out, out_sem.at[3])
     total_copy.start()
 
     for copy in sent:
         copy.wait_send()
     pltpu.make_async_copy(three, three, sum_send.at[0]).wait()
+    pltpu.make_async_copy(others, others, sum_send.at[3]).wait()
     pltpu.make_async_copy(many, many, sum_send.at[1]).wait()
     pltpu.make_async_copy(some, some, sum_send.at[2]).wait()
     for copy in bases_out:
@@ -369,14 +383,15 @@
             pltpu.VMEM((early, 1, LANES), jnp.float32),
             pltpu.VMEM((rows_p, 1, LANES), jnp.float32),
             pltpu.VMEM((ny, quarter, 1, LANES), jnp.float32),
-            pltpu.VMEM((nz, 16, LANES), jnp.bfloat16),
-            pltpu.VMEM((ny, 16, LANES), jnp.float32),
+            pltpu.VMEM((ny, rows_p // ny, 1, LANES), jnp.float32),
+            pltpu.VMEM((nz, rows // ny, LANES), jnp.bfloat16),
+            pltpu.VMEM((ny, rows // ny, LANES), jnp.float32),
             pltpu.VMEM((rows, 1, LANES), jnp.float32),
             pltpu.SemaphoreType.DMA((5,)),
             pltpu.SemaphoreType.DMA((13,)),
             pltpu.SemaphoreType.DMA((13,)),
-            pltpu.SemaphoreType.DMA((3,)),
-            pltpu.SemaphoreType.DMA((3,)),
+            pltpu.SemaphoreType.DMA((4,)),
+            pltpu.SemaphoreType.DMA((4,)),
             pltpu.SemaphoreType.DMA((4,)),
             pltpu.SemaphoreType.REGULAR(((nz // 2).bit_length() - 2,)),
             pltpu.SemaphoreType.REGULAR(((nz // 2).bit_length() - 2,)),

time: 53.9 us -> 52 us (0.965)
  the two profiles are of different devices: /device:TPU:2 before, /device:TPU:32 now
where the time goes in v5:
time: 52 us; the launch traced here: 51.9 us
  Pallas kernels  51.2 us (98%)
  between operations  0.67 us (1%)
    pallas_call x1, Pallas kernels, shards(): pl.pallas_call(functools.partial(first_kernel, ny, nz), out_shape=(pltpu....  49.6 us
    pallas_call x1, Pallas kernels, shards(): pl.pallas_call(second_kernel, out_shape=(jax.ShapeDtypeStruct((feats, wid...  1.63 us

profile of v5, /device:TPU:32, one launch (start us, length us, event | category | flops | bytes accessed | tf_op | source)
XLA Modules:
  0.0 51.9 jit_solution(84821127173697395)
XLA Ops:
  0.6 0.0 copy-start.1
  0.6 0.0 copy-start
  0.7 49.6 %gather_encode_sum.1 = (f32[512,512]{1,0:T(8,128)S(1)}, f32[32,1,128]{2,1,0:T(1,128)S(1)}, f32[8,64,512]{2,1,0:T(8,128)S(1)}, bf16[8,4,128,256]{3,2,1,0:T(8,128)(2,1)S(1)}) custom-call(bf16[1024,512]{1,0:T(8,128)(2,1)} %tok_hbm.1, bf16[64,1024]{1,0:T(8,128)(2,1)} %bitcast.5, f32[512,512]{1,0:T(8,128)} %bitcast.3, s32[8,8,64]{2,1,0:T(8,128)} %pos_hbm.1, ...), custom_call_target="tpu_custom_call" | custom-call | flops 1000000000 | bytes 8000000 | tf_op jit(solution)/shard_map/gather_encode_sum/pallas_call | solution.py:364
  50.3 0.0 copy-done.1
  50.3 0.0 copy-done
  50.3 1.6 %decode_blend.1 = (f32[512,512]{1,0:T(8,128)}, f32[512,512]{1,0:T(8,128)}, bf16[512,512]{1,0:T(8,128)(2,1)}) custom-call(f32[32,1,128]{2,1,0:T(1,128)S(1)} %get-tuple-element.10.total, f32[8,64,512]{2,1,0:T(8,128)S(1)} %get-tuple-element.11.at, bf16[8,4,128,256]{3,2,1,0:T(8,128)(2,1)S(1)} %get-tuple-element.12.w, f32[512,512]{1,0:T(8,128)S(1)} %get-tuple-element.13.res_in, ...), custom_call_target="tpu_custom_call" | custom-call | flops 300000000 | bytes 8000000 | tf_op jit(solution)/shard_map/decode_blend/pallas_call | solution.py:406
Async XLA Ops:
  0.6 49.6 %copy-start.1 = (bf16[512,512]{1,0:T(8,128)(2,1)S(1)}, bf16[512,512]{1,0:T(8,128)(2,1)}, u32[]{:S(2)}) copy-start(bf16[512,512]{1,0:T(8,128)(2,1)} %target.1) | copy-start | bytes 1572868
  0.6 49.6 %copy-start = (bf16[512,512]{1,0:T(8,128)(2,1)S(1)}, bf16[512,512]{1,0:T(8,128)(2,1)}, u32[]{:S(2)}) copy-start(bf16[512,512]{1,0:T(8,128)(2,1)} %weight.1) | copy-start | bytes 1572868

commit v6 on v5

--- a/solution.py
+++ b/solution.py
@@ -85,7 +85,7 @@
     tok_hbm, grad_hbm, mom_hbm, pos_hbm, table_hbm,
     res_out, total_out, at_out, w_out,
     tok, tok_t, gall, mom, at, w, pos, table, early, late, y_parts, y_lasts, z_parts, y_sums, total,
-    load_sem, send_sem, recv_sem, sum_send, sum_recv, out_sem, know_down, know_up,
+    load_sem, send_sem, recv_sem, sum_send, sum_recv, out_sem, know_y, know_down, know_up,
 ):
     rep, tp = lax.axis_index("rep"), lax.axis_index("tp")
     z, y = rep // ny, lax.rem(rep, ny)
@@ -120,21 +120,20 @@
     barrier = pltpu.get_barrier_semaphore()
     for peer in (right, left, other):
         tell(barrier, {"tp": peer})
-    for step in (2, -2, 1, -1):
+    for step in (1, -1):
         tell(barrier, z_peer(step))
-    for step in range(1, ny):
         tell(barrier, y_peer(step))
     for number in (3, 4, 0, 1):
         loads[number].start()
 
     loads[2].wait()
-    pl.semaphore_wait(barrier, 3 + 4 + ny - 1)
+    pl.semaphore_wait(barrier, 7)
 
     levels = know_down.shape[0]
 
     def pass_on(level):
-        tell(know_down.at[level], z_peer(2 << level))
-        tell(know_up.at[level], z_peer(-(2 << level)))
+        tell(know_down.at[level], z_peer(1 << level))
+        tell(know_up.at[level], z_peer(-(1 << level)))
 
     def learn(level):
         pl.semaphore_wait(know_down.at[level], 1)
@@ -142,6 +141,7 @@
         if level + 1 < levels:
             pass_on(level + 1)
 
+    tell(know_y, y_peer(-1))
     pass_on(0)
     half = BLOCK // 2
 
@@ -175,6 +175,8 @@
     for at_row in range(0, depth, 256):
         tok_t[:, at_row : at_row + 256] = tok[at_row : at_row + 256, :].T
     loads[4].wait()
+    pl.semaphore_wait(know_y, 1)
+    learn(0)
     loads[0].wait()
     loads[1].wait()
     make_bases(pos, table, at, w)
@@ -184,7 +186,7 @@
     ]
     for copy in bases_out:
         copy.start()
-    learn(0)
+    learn(1)
 
     arrived(0, rows(left, 0))
     sent.append(send(4, rows(left, 0), right))
@@ -219,11 +221,11 @@
 
     arrived(6, gall.at[pl.ds(pl.multiple_of(other * BLOCK, BLOCK), BLOCK)])
     forward(x, early, 0)
-    for level in range(1, levels - 1):
-        learn(level)
     arrived(7, rows(left_o, 0))
     arrived(8, rows(left_o, 1))
     forward(left_x, early, rows_p)
+    for level in range(2, levels - 1):
+        learn(level)
     arrived(9, rows(right_o, 0))
     arrived(10, rows(right_o, 1))
     forward(right_x, early, 2 * rows_p)
@@ -393,8 +395,9 @@
             pltpu.SemaphoreType.DMA((4,)),
             pltpu.SemaphoreType.DMA((4,)),
             pltpu.SemaphoreType.DMA((4,)),
-            pltpu.SemaphoreType.REGULAR(((nz // 2).bit_length() - 2,)),
-            pltpu.SemaphoreType.REGULAR(((nz // 2).bit_length() - 2,)),
+            pltpu.SemaphoreType.REGULAR,
+            pltpu.SemaphoreType.REGULAR(((nz // 2).bit_length() - 1,)),
+            pltpu.SemaphoreType.REGULAR(((nz // 2).bit_length() - 1,)),
         ],
         compiler_params=pltpu.CompilerParams(
             collective_id=0, has_side_effects=True, vmem_limit_bytes=54 * 1024 * 1024

time: 52 us -> 51.8 us (level)
  the two profiles are of different devices: /device:TPU:32 before, /device:TPU:8 now
where the time goes in v6:
time: 51.8 us; the launch traced here: 51.6 us
  Pallas kernels  50.9 us (98%)
  between operations  0.67 us (1%)
    pallas_call x1, Pallas kernels, shards(): pl.pallas_call(functools.partial(first_kernel, ny, nz), out_shape=(pltpu....  49.3 us
    pallas_call x1, Pallas kernels, shards(): pl.pallas_call(second_kernel, out_shape=(jax.ShapeDtypeStruct((feats, wid...  1.63 us

profile of v6, /device:TPU:8, one launch (start us, length us, event | category | flops | bytes accessed | tf_op | source)
XLA Modules:
  0.0 51.6 jit_solution(1068006163711151996)
XLA Ops:
  0.6 0.0 copy-start.1
  0.6 0.0 copy-start
  0.7 49.3 %gather_encode_sum.1 = (f32[512,512]{1,0:T(8,128)S(1)}, f32[32,1,128]{2,1,0:T(1,128)S(1)}, f32[8,64,512]{2,1,0:T(8,128)S(1)}, bf16[8,4,128,256]{3,2,1,0:T(8,128)(2,1)S(1)}) custom-call(bf16[1024,512]{1,0:T(8,128)(2,1)} %tok_hbm.1, bf16[64,1024]{1,0:T(8,128)(2,1)} %bitcast.5, f32[512,512]{1,0:T(8,128)} %bitcast.3, s32[8,8,64]{2,1,0:T(8,128)} %pos_hbm.1, ...), custom_call_target="tpu_custom_call" | custom-call | flops 1000000000 | bytes 8000000 | tf_op jit(solution)/shard_map/gather_encode_sum/pallas_call | solution.py:366
  50.0 0.0 copy-done.1
  50.0 0.0 copy-done
  50.0 1.6 %decode_blend.1 = (f32[512,512]{1,0:T(8,128)}, f32[512,512]{1,0:T(8,128)}, bf16[512,512]{1,0:T(8,128)(2,1)}) custom-call(f32[32,1,128]{2,1,0:T(1,128)S(1)} %get-tuple-element.10.total, f32[8,64,512]{2,1,0:T(8,128)S(1)} %get-tuple-element.11.at, bf16[8,4,128,256]{3,2,1,0:T(8,128)(2,1)S(1)} %get-tuple-element.12.w, f32[512,512]{1,0:T(8,128)S(1)} %get-tuple-element.13.res_in, ...), custom_call_target="tpu_custom_call" | custom-call | flops 300000000 | bytes 8000000 | tf_op jit(solution)/shard_map/decode_blend/pallas_call | solution.py:409
Async XLA Ops:
  0.6 49.3 %copy-start.1 = (bf16[512,512]{1,0:T(8,128)(2,1)S(1)}, bf16[512,512]{1,0:T(8,128)(2,1)}, u32[]{:S(2)}) copy-start(bf16[512,512]{1,0:T(8,128)(2,1)} %target.1) | copy-start | bytes 1572868
  0.6 49.3 %copy-start = (bf16[512,512]{1,0:T(8,128)(2,1)S(1)}, bf16[512,512]{1,0:T(8,128)(2,1)}, u32[]{:S(2)}) copy-start(bf16[512,512]{1,0:T(8,128)(2,1)} %weight.1) | copy-start | bytes 1572868
